TPU v7x, 256 devices: a whole 4x4x8 slice. The times are simulated.
256 devices in a mesh: kv: 32 (over z, y), seq: 8 (over x, core).
Axes of the slice: x: 4, y: 4, z: 8, core: 2. Of those that a mesh axis runs over, the one named last changes fastest.
Arguments:
- kv_cache: bfloat16 [32, 73728, 576], P('seq', 'kv'), may hold values from -4 to 4
- lengths: int32 [32], P('seq'), may hold values from 4608 to 73728, as said below
- q_nope: bfloat16 [32, 128, 128], P('seq', 'kv'), may hold values from -6 to 6
- q_rope: bfloat16 [32, 128, 64], P('seq', 'kv'), may hold values from -32 to 32
- w_uk: bfloat16 [128, 128, 512], P('kv'), may hold values from -0.75 to 0.75
- w_uv: bfloat16 [128, 512, 128], P('kv'), may hold values from -3 to 3
- w_o: bfloat16 [16384, 7168], P('kv', 'seq'), may hold values from -0.046875 to 0.046875
Outputs:
- layer_out: bfloat16 [32, 7168], P('kv', 'seq')
Inputs may be any that keep to these rules, and one draw needn't show every extreme that they name: `lengths`: at least one sequence has all 73728 slots live.
All inputs are finite; a program needn't handle non-finite values.
Results may differ from a plain program's by a relative error of at most 0.025.
Values may be sent and summed in bfloat16 or wider, within the bound.
A program may use at most 64 MiB of HBM per device.

v0:
```python
import math

import jax
import jax.numpy as jnp
from jax import lax
from jax.sharding import PartitionSpec as P


def per_device(kv_cache, lengths, q_nope, q_rope, w_uk, w_uv, w_o):
    seq_dev, ctx_dev, latent_width = kv_cache.shape
    latent_rank = w_uv.shape[1]
    score_scale = 1.0 / math.sqrt(q_nope.shape[2] + q_rope.shape[2])
    absorbed = jnp.einsum("bhn,hnr->bhr", q_nope, w_uk, preferred_element_type=jnp.float32).astype(
        jnp.bfloat16
    )
    all_absorbed, all_rope = (
        lax.all_gather(absorbed, "kv", axis=1, tiled=True),
        lax.all_gather(q_rope, "kv", axis=1, tiled=True),
    )
    queries = jnp.concatenate([all_absorbed, all_rope], axis=-1)
    first_slot = lax.axis_index("kv") * ctx_dev
    positions = first_slot + lax.broadcasted_iota(jnp.int32, (seq_dev, ctx_dev), 1)
    live_mask = positions < lengths[:, None]
    scores = (
        jnp.einsum("bhl,btl->bht", queries, kv_cache, preferred_element_type=jnp.float32)
        * score_scale
    )
    scores = jnp.where(live_mask[:, None, :], scores, -1e30)
    maxima = jnp.max(scores, axis=-1)
    weights = jnp.where(live_mask[:, None, :], jnp.exp(scores - maxima[..., None]), 0.0)
    totals = jnp.sum(weights, axis=-1)
    partial_out = jnp.einsum(
        "bht,btl->bhl", weights.astype(jnp.bfloat16), kv_cache, preferred_element_type=jnp.float32
    )[..., :latent_rank]
    normalized = (partial_out / jnp.maximum(totals, 1.0)[..., None]).astype(jnp.bfloat16)
    gathered_parts = lax.all_to_all(normalized[None], "kv", split_axis=2, concat_axis=0, tiled=True)
    gathered_maxima, gathered_totals = (
        lax.all_to_all(maxima[None], "kv", split_axis=2, concat_axis=0, tiled=True),
        lax.all_to_all(totals[None], "kv", split_axis=2, concat_axis=0, tiled=True),
    )
    largest = jnp.max(gathered_maxima, axis=0)
    factors = jnp.exp(gathered_maxima - largest) * gathered_totals
    summed = jnp.sum(factors, axis=0)
    latent = (
        jnp.sum(factors[..., None] * gathered_parts.astype(jnp.float32), axis=0) / summed[..., None]
    ).astype(jnp.bfloat16)
    heads_out = jnp.einsum("bhr,hrv->bhv", latent, w_uv, preferred_element_type=jnp.float32).astype(
        jnp.bfloat16
    )
    heads_out = heads_out.reshape(seq_dev, -1)
    all_heads = lax.all_gather(heads_out, "seq", axis=0, tiled=True)
    return lax.psum_scatter(
        jnp.dot(all_heads, w_o, preferred_element_type=jnp.float32).astype(jnp.bfloat16),
        "kv",
        scatter_dimension=0,
        tiled=True,
    )


def solution(mesh):
    return jax.shard_map(
        per_device,
        mesh=mesh,
        in_specs=(
            P("seq", "kv", None),
            P("seq"),
            P("seq", "kv", None),
            P("seq", "kv", None),
            P("kv", None, None),
            P("kv", None, None),
            P("kv", "seq"),
        ),
        out_specs=P("kv", "seq"),
        check_vma=False,
    )
```

profile of v0, /device:TPU:2, one launch (start us, length us, event | category | flops | bytes accessed | tf_op | source)
XLA Modules:
  0.0 315.4 jit_solution(4771661023604752651)
XLA Ops:
  0.0 0.0 copy-start
  0.0 0.8 copy.22
  0.8 46.6 %all_gather.10 = bf16[4,128,64]{2,0,1:T(4,128)(2,1)S(1)} all-gather(bf16[4,4,64]{2,0,1:T(4,128)(2,1)S(1)} %copy.22), channel_id=1, replica_groups=mesh['kv'=32,'seq'=8] {'kv'}, dimensions={1}, use_global_device_ids=true | all-gather | bytes 67584 | tf_op jit(solution)/shard_map/all_gather | solution.py:18
  47.4 0.1 copy.24
  47.5 1.2 fusion.9
  48.7 48.3 %all_gather.9 = bf16[4,128,512]{2,0,1:T(4,128)(2,1)S(1)} all-gather(bf16[4,4,512]{2,0,1:T(4,128)(2,1)S(1)} %fusion.9), channel_id=1, replica_groups=mesh['kv'=32,'seq'=8] {'kv'}, dimensions={1}, use_global_device_ids=true | all-gather | bytes 540672 | tf_op jit(solution)/shard_map/all_gather | solution.py:17
  97.0 0.4 copy.23
  97.5 0.7 broadcast_compare_fusion
  98.2 6.4 %fusion.30 = (f32[4,128]{1,0:T(4,128)S(1)}, f32[4,128,2304]{2,1,0:T(8,128)S(1)}) fusion(bf16[4,2304,576]{1,2,0:T(8,128)(2,1)} %param.7, bf16[4,128,64]{1,2,0:T(8,128)(2,1)S(1)} %copy.24, bf16[4,128,512]{1,2,0:T(8,128)(2,1)S(1)} %copy.23, pred[4,2304]{1,0:T(4,128)(4,1)S(1)} %broadcast_compare_fusion), kind=kOutput, calls=%fused_computation.36 | convolution fusion | flops 1363672576 | bytes 15936512 | tf_op jit(solution)/shard_map/bhl,btl->bht/dot_general | solution.py:25
  104.6 0.0 copy-start.1
  104.6 2.1 copy-done.1
  106.7 1.0 fusion.4
  107.7 0.7 copy.27
  108.5 6.1 %all-to-all-start.1 = ((f32[1,4,128]{1,0,2:T(1,128)}), f32[1,4,128]{1,0,2:T(1,128)S(1)}, u32[]{:S(2)}, u32[]{:S(2)}) async-start(f32[1,4,128]{1,0,2:T(1,128)} %copy.27), calls=%async_computation.1 | async-start | bytes 131072 | tf_op jit(solution)/shard_map/all_to_all | solution.py:39
  114.6 0.7 copy.25
  115.3 9.2 %all-to-all-done.1 = f32[1,4,128]{1,0,2:T(1,128)S(1)} async-done(((f32[1,4,128]{1,0,2:T(1,128)}), f32[1,4,128]{1,0,2:T(1,128)S(1)}, u32[]{:S(2)}, u32[]{:S(2)}) %all-to-all-start.1) | async-done | bytes 2080 | tf_op jit(solution)/shard_map/all_to_all | solution.py:39
  124.6 3.8 %all-to-all-start = ((f32[1,4,128]{1,0,2:T(1,128)}), f32[1,4,128]{1,0,2:T(1,128)S(1)}, u32[]{:S(2)}, u32[]{:S(2)}) async-start(f32[1,4,128]{1,0,2:T(1,128)} %copy.25), calls=%async_computation | async-start | bytes 131072 | tf_op jit(solution)/shard_map/all_to_all | solution.py:38
  128.4 0.0 copy-start.3
  128.4 8.4 %fusion.16 = bf16[1,4,128,512]{3,2,1,0:T(8,128)(2,1)S(1)} fusion(bf16[4,2304,576]{1,2,0:T(8,128)(2,1)} %param.7, f32[4,128,2304]{2,1,0:T(8,128)} %copy-done.1, f32[4,128]{1,0:T(4,128)S(1)} %get-tuple-element.7, pred[4,2304]{1,0:T(4,128)(4,1)S(1)} %broadcast_compare_fusion, f32[4,128]{1,0:T(4,128)S(1)} %broadcast_maximum_fusion), kind=kOutput, calls=%fused_computation.18 | convolution fusion | flops 1212022784 | bytes 14693376 | tf_op jit(solution)/shard_map/bht,btl->bhl/dot_general | solution.py:32
  136.8 0.0 copy-start.2
  136.8 1.2 copy.29
  138.0 0.4 all-to-all-done
  138.4 9.3 %all-to-all-start.2 = ((bf16[1,4,128,512]{3,1,0,2:T(4,128)(2,1)}), bf16[1,4,128,512]{3,1,0,2:T(4,128)(2,1)S(1)}, u32[]{:S(2)}, u32[]{:S(2)}) async-start(bf16[1,4,128,512]{3,1,0,2:T(4,128)(2,1)} %copy.29), calls=%async_computation.2 | async-start | bytes 1048576 | tf_op jit(solution)/shard_map/all_to_all | solution.py:36
  147.8 0.0 copy-done.3
  147.8 0.7 dynamic-slice
  148.5 0.3 copy.33
  148.8 0.3 copy.32
  149.2 12.4 %all-to-all-done.2 = bf16[1,4,128,512]{3,1,0,2:T(4,128)(2,1)S(1)} async-done(((bf16[1,4,128,512]{3,1,0,2:T(4,128)(2,1)}), bf16[1,4,128,512]{3,1,0,2:T(4,128)(2,1)S(1)}, u32[]{:S(2)}, u32[]{:S(2)}) %all-to-all-start.2) | async-done | bytes 524320 | tf_op jit(solution)/shard_map/all_to_all | solution.py:36
  161.6 0.1 convert.3
  161.8 0.5 fusion.11
  162.2 0.1 divide_convert_fusion.1
  162.3 0.0 copy-done.2
  162.3 0.2 fusion.10
  162.5 12.8 %all-gather = bf16[8,4,512]{2,1,0:T(4,128)(2,1)S(1)} all-gather(bf16[1,4,512]{2,1,0:T(4,128)(2,1)S(1)} %fusion.10), channel_id=1, replica_groups=mesh['kv'=32,'seq'=8] {'seq'}, dimensions={0}, use_global_device_ids=true | all-gather | bytes 36864 | tf_op jit(solution)/shard_map/all_gather | solution.py:51
  175.4 0.0 copy-done
  175.4 0.3 convolution_convert_fusion
  175.6 138.5 %all-reduce = bf16[32,896]{1,0:T(8,128)(2,1)S(1)} all-reduce(bf16[32,896]{1,0:T(8,128)(2,1)S(1)} %convolution_convert_fusion), channel_id=2, replica_groups=mesh['kv'=32,'seq'=8] {'kv'}, use_global_device_ids=true, to_apply=%region_5.6.clone | all-reduce | flops 28672 | bytes 114688
  314.2 1.3 constant_dynamic-slice_fusion
  (5 shorter events, 0.1 us)
Async XLA Ops:
  0.0 175.4 %copy-start = (bf16[512,896]{1,0:T(8,128)(2,1)S(1)}, bf16[512,896]{1,0:T(8,128)(2,1)}, u32[]{:S(2)}) copy-start(bf16[512,896]{1,0:T(8,128)(2,1)} %param.13) | copy-start | bytes 2752516
  104.6 2.1 copy-start.1
  108.5 16.1 %all-to-all-start.1 = ((f32[1,4,128]{1,0,2:T(1,128)}), f32[1,4,128]{1,0,2:T(1,128)S(1)}, u32[]{:S(2)}, u32[]{:S(2)}) async-start(f32[1,4,128]{1,0,2:T(1,128)} %copy.27), calls=%async_computation.1 | async-start | bytes 131072 | tf_op jit(solution)/shard_map/all_to_all | solution.py:39
  124.6 13.9 %all-to-all-start = ((f32[1,4,128]{1,0,2:T(1,128)}), f32[1,4,128]{1,0,2:T(1,128)S(1)}, u32[]{:S(2)}, u32[]{:S(2)}) async-start(f32[1,4,128]{1,0,2:T(1,128)} %copy.25), calls=%async_computation | async-start | bytes 131072 | tf_op jit(solution)/shard_map/all_to_all | solution.py:38
  128.4 19.4 %copy-start.3 = (u32[256]{0:T(256)S(1)}, u32[256]{0:T(256)}, u32[]{:S(2)}) copy-start(u32[256]{0:T(256)} %constant.26) | copy-start | bytes 3076
  136.8 25.6 %copy-start.2 = (bf16[4,512,128]{2,1,0:T(8,128)(2,1)S(1)}, bf16[4,512,128]{2,1,0:T(8,128)(2,1)}, u32[]{:S(2)}) copy-start(bf16[4,512,128]{2,1,0:T(8,128)(2,1)} %param.12) | copy-start | bytes 1572868
  138.4 23.2 %all-to-all-start.2 = ((bf16[1,4,128,512]{3,1,0,2:T(4,128)(2,1)}), bf16[1,4,128,512]{3,1,0,2:T(4,128)(2,1)S(1)}, u32[]{:S(2)}, u32[]{:S(2)}) async-start(bf16[1,4,128,512]{3,1,0,2:T(4,128)(2,1)} %copy.29), calls=%async_computation.2 | async-start | bytes 1048576 | tf_op jit(solution)/shard_map/all_to_all | solution.py:36
where the time goes:
time: 316 us; the launch traced here: 315 us
  blocking collectives  246 us (78%)
  waiting for transfers between devices  22.1 us (7%)
  starting transfers between devices  19.3 us (6%)
  matrix products  16.4 us (5%)
  local copies, waits for them, and re-layouts  8.72 us (3%)
    unnamed x1, blocking collectives  139 us
    all_gather x1, blocking collectives, per_device(): lax.all_gather(absorbed, 'kv', axis=1, tiled=True)  48.3 us
    all_gather x1, blocking collectives, per_device(): lax.all_gather(q_rope, 'kv', axis=1, tiled=True)  46.6 us
    all_gather x1, blocking collectives, per_device(): all_heads = lax.all_gather(heads_out, 'seq', axis=0, tiled=True)  12.8 us
    all_to_all x1, waiting for transfers between devices, per_device(): lax.all_to_all(normalized[None], 'kv', split_axis=2, concat_axis=0, tiled...  12.4 us
    all_to_all x1, starting transfers between devices, per_device(): lax.all_to_all(normalized[None], 'kv', split_axis=2, concat_axis=0, tiled...  9.35 us
    all_to_all x1, waiting for transfers between devices, per_device(): lax.all_to_all(totals[None], 'kv', split_axis=2, concat_axis=0, tiled=True)  9.23 us
    dot_general x1, matrix products, per_device(): jnp.einsum('bht,btl->bhl', weights.astype(jnp.bfloat16), kv_cache, prefer...  8.36 us
  transfers between devices with their start and end apart: 3, of which 3 were waited for; matrix products, arithmetic and copies ran while one was open for 4% of the time, Pallas kernels for 0%

commit v1 on v0

v1 whole, which is shorter than its diff:
```python
import functools
import math

import jax
import jax.numpy as jnp
from jax import lax
from jax.experimental import pallas as pl
from jax.experimental.pallas import tpu as pltpu
from jax.sharding import PartitionSpec as P

F32 = jnp.float32
BF16 = jnp.bfloat16
NZ, NY, NS = 8, 4, 8
B, HL = 4, 4
LAST = B - 1
SEQS = NS * B
RANK, ROPE, NOPE, VH = 512, 64, 128, 128
ROWS = B * HL
GROUP = NZ * HL
HEADS = NY * GROUP
LANES = 128
PARTS = RANK // LANES
DEAD, FLOOR = -1e30, -1e29
FAR_FIRST = sorted(range(1, NZ), key=lambda d: (-min(d, NZ - d), d))


def halves(a, c):
    first = lax.broadcasted_iota(jnp.int32, a.shape, 0) < 4
    return (
        jnp.where(first, a, pltpu.roll(c, 4, 0)),
        jnp.where(first, pltpu.roll(a, 4, 0), c),
    )


def take(block, lane):
    return jnp.broadcast_to(block[:, lane:lane + 1], block.shape)


def kernel(
    lengths_hbm, qn_hbm, qr_hbm, kv_hbm, wuk_hbm, wuv_hbm, wo_hbm, out,
    lengths, qn, qr, kvt, vt, wuk, wuv, wo,
    own, g1, g1r, ya, za, spread, around, qall, qrope, qrope3, d1s, d1, tall, t1s, t1, factor, flat, d2s, d2, t2s, t2, deep,
    lat, fall, ff, wide, h2s, h2,
    local, local_kv, sent, r_g1, r_g2, r_a, r_d1, r_t1, r_d2, r_t2, r_f, r_h2,
):
    kv, s = lax.axis_index("kv"), lax.axis_index("seq")
    z, y = kv // NY, kv % NY
    ctx = kvt.shape[2]
    scale = 1.0 / math.sqrt(NOPE + ROPE)

    def at_z(i):
        return {"kv": i * NY + y, "seq": s}

    def at_y(i):
        return {"kv": z * NY + i, "seq": s}

    def at_s(i):
        return {"kv": kv, "seq": i}

    def zs(d):
        return lax.rem(z + d, NZ)

    def ys(d):
        return lax.rem(y + d, NY)

    def ss(d):
        return lax.rem(s + d, NS)

    barrier = pltpu.get_barrier_semaphore()
    peers = (
        [at_z(zs(d)) for d in FAR_FIRST]
        + [at_s(ss(d)) for d in range(1, NS)]
        + [at_y(ys(d)) for d in range(1, NY)]
    )
    for peer in peers:
        pl.semaphore_signal(barrier, inc=1, device_id=peer, device_id_type=pl.DeviceIdType.MESH)

    small = [
        pltpu.make_async_copy(qn_hbm, qn, local.at[0]),
        pltpu.make_async_copy(qr_hbm, qr, local.at[1]),
        pltpu.make_async_copy(wuk_hbm, wuk, local.at[2]),
    ]
    late = [
        pltpu.make_async_copy(wuv_hbm, wuv, local.at[3]),
        pltpu.make_async_copy(wo_hbm, wo, local.at[4]),
        pltpu.make_async_copy(lengths_hbm, lengths, local.at[5]),
    ]
    caches = [
        pltpu.make_async_copy(kv_hbm.at[b], kvt.at[b], local_kv.at[b]) for b in range(B)
    ]
    for copy in small:
        copy.start()

    def send(src, dst, send_sem, recv_sem, to):
        pltpu.make_async_remote_copy(
            src_ref=src, dst_ref=dst, send_sem=send_sem, recv_sem=recv_sem,
            device_id=to, device_id_type=pl.DeviceIdType.MESH,
        ).start()

    def bytes_of(ref, sem):
        return pltpu.make_async_remote_copy(
            src_ref=ref, dst_ref=ref, send_sem=sem, recv_sem=sem,
            device_id=at_z(z), device_id_type=pl.DeviceIdType.MESH,
        )

    def arrive(ref, sem):
        bytes_of(ref, sem).wait_recv()

    def yrows(i):
        return pl.ds(pl.multiple_of(i * GROUP, GROUP), GROUP)

    for copy in small:
        copy.wait()
    for copy in caches + late:
        copy.start()
    head = lax.broadcasted_iota(jnp.int32, (ROWS, 1), 0) % HL
    q16 = qn[...].astype(F32).reshape(ROWS, NOPE).astype(BF16)
    absorbed = jnp.zeros((ROWS, RANK), F32)
    for h in range(HL):
        product = jnp.dot(q16, wuk[h], preferred_element_type=F32)
        absorbed = jnp.where(head == h, product, absorbed)
    rope = qr[...].astype(F32).reshape(ROWS, ROPE)
    for j in range(PARTS):
        own[pl.ds(j, ROWS, stride=PARTS)] = absorbed[:, j * LANES:(j + 1) * LANES]
    g1[z] = own[...].astype(BF16).reshape(B, HL * PARTS, LANES)
    ya[y, 0] = g1[z, LAST]
    g1r[z] = jnp.concatenate([rope, jnp.zeros((ROWS, LANES - ROPE), F32)], axis=1).astype(BF16)
    ya[y, 1] = g1r[z]

    pl.semaphore_wait(barrier, len(peers))

    for d in FAR_FIRST:
        send(g1.at[z, 0], g1.at[z, 0], sent.at[1], r_g1.at[1], at_z(zs(d)))
    for d in (2, 1, 3):
        send(ya.at[y], ya.at[y], sent.at[10], r_a.at[0], at_y(ys(d)))
    for d in FAR_FIRST:
        send(g1r.at[z], g1r.at[z], sent.at[0], r_g1.at[0], at_z(zs(d)))
    for d in FAR_FIRST:
        rest = g1.at[z, pl.ds(1, LAST - 1)]
        send(rest, rest, sent.at[1], r_g1.at[2], at_z(zs(d)))

    def turn_cache(b):
        caches[b].wait()
        vt[b] = kvt[b, :RANK].T

    def pass_on(b):
        spread[b] = g1[:, b].astype(F32).reshape(GROUP * PARTS, LANES)
        parts = [spread[b, pl.ds(j, GROUP, stride=PARTS)] for j in range(PARTS)]
        part = qall.at[b, yrows(y)]
        part[...] = jnp.concatenate(parts, axis=1).astype(BF16)
        for d in (2, 1, 3):
            send(part, part, sent.at[2], r_g2.at[b], at_y(ys(d)))

    turn_cache(0)
    arrive(ya.at[pl.ds(1, NY - 1)], r_a.at[0])
    around[...] = ya[:, 0].astype(F32).reshape(NY * ROWS, LANES)
    parts = [around[pl.ds(j, ROWS, stride=PARTS)] for j in range(PARTS)]
    tails = [ya[i, 1].astype(F32)[8:] for i in range(NY)]
    tail = jnp.concatenate(
        [halves(tails[0], tails[1])[1], halves(tails[2], tails[3])[1]], axis=0
    )
    za[z] = jnp.concatenate(parts + [tail], axis=1).astype(BF16)
    for d in FAR_FIRST:
        send(za.at[z], za.at[z], sent.at[11], r_a.at[1], at_z(zs(d)))
    turn_cache(1)
    arrive(g1.at[pl.ds(1, NZ - 1), 0], r_g1.at[1])
    pass_on(0)
    arrive(g1r.at[pl.ds(1, NZ - 1)], r_g1.at[0])
    for k in range(0, NZ, 4):
        blocks = [g1r[k + j].astype(F32) for j in range(4)]
        for p in range(B // 2):
            rows = slice(8 * p, 8 * p + 8)
            low = halves(blocks[0][rows], blocks[1][rows])
            high = halves(blocks[2][rows], blocks[3][rows])
            pair = [jnp.concatenate([low[i], high[i]], axis=0) for i in range(2)]
            where = pl.ds(pl.multiple_of(y * GROUP + k * HL, 16), 16)
            both = pair[0] + pltpu.roll(pair[1], ROPE, 1)
            qrope[where, p * LANES:(p + 1) * LANES] = both.astype(BF16)
    part = qrope.at[yrows(y)]
    for d in (2, 1, 3):
        send(part, part, sent.at[3], r_g2.at[LAST], at_y(ys(d)))
    arrive(g1.at[pl.ds(1, NZ - 1), pl.ds(1, LAST - 1)], r_g1.at[2])
    for b in range(1, LAST):
        pass_on(b)

    for b in range(2, B):
        turn_cache(b)

    def turn():
        arrive(za.at[pl.ds(1, NZ - 1)], r_a.at[1])
        for k in range(0, NZ, 4):
            blocks = [za[k + j].astype(F32) for j in range(4)]
            for p in range(NY // 2):
                rows = slice(8 * p, 8 * p + 8)
                low = halves(blocks[0][rows], blocks[1][rows])
                high = halves(blocks[2][rows], blocks[3][rows])
                for i in range(2):
                    both = jnp.concatenate([low[i], high[i]], axis=0).astype(BF16)
                    first = (2 * p + i) * GROUP + k * HL
                    qall[LAST, first:first + 16] = both[:, :RANK]
                    qrope3[first:first + 16] = both[:, RANK:]

    even = lax.broadcasted_iota(jnp.int32, (NZ, LANES), 1) % 2 == 0

    def pack(b, maxima, totals):
        lane = lax.broadcasted_iota(jnp.int32, (HEADS, LANES), 1)
        tall[b] = jnp.where(lane == 0, maxima, jnp.where(lane == 1, totals, 0.0))
        for i in range(NY):
            block = tall[b, pl.ds(i * GROUP, NZ, stride=HL)]
            for h in range(1, HL):
                block = block + pltpu.roll(tall[b, pl.ds(i * GROUP + h, NZ, stride=HL)], 2 * h, 1)
            t1s[b, i] = block

    def join(b):
        t1[b, y] = t1s[b, y]
        d1[b, y] = d1s[b, yrows(y)]
        arrive(t1.at[b, pl.ds(1, NY - 1)], r_t1.at[b])
        stats = [t1[b, i] for i in range(NY)]
        largest = functools.reduce(jnp.maximum, stats)
        factors = [jnp.exp(t - largest) * pltpu.roll(t, LANES - 1, 1) for t in stats]
        summed = sum(factors)
        inverse = 1.0 / jnp.maximum(summed, 1.0)
        joined = jnp.where(even, largest, pltpu.roll(summed, 1, 1))
        for i in range(NZ):
            t2s[b, i] = joined[i:i + 1]
        for d in FAR_FIRST:
            i = zs(d)
            send(t2s.at[b, i], t2.at[b, z], sent.at[7], r_t2.at[b], at_z(i))
        for i in range(NY):
            share = factors[i] * inverse
            for h in range(HL):
                factor[b, i, pl.ds(h, NZ, stride=HL)] = take(share, 2 * h)
        arrive(d1.at[b, pl.ds(1, NY - 1)], r_d1.at[b])
        total = 0.0
        for i in range(NY):
            share = jnp.concatenate([factor[b, i]] * PARTS, axis=1)
            total = total + share * d1[b, i].astype(F32)
        for j in range(PARTS):
            flat[b, pl.ds(j, GROUP, stride=PARTS)] = total[:, j * LANES:(j + 1) * LANES]
        d2s[b] = flat[b].astype(BF16).reshape(NZ, ROWS, LANES)
        for d in FAR_FIRST:
            i = zs(d)
            send(d2s.at[b, i], d2.at[b, z], sent.at[6], r_d2.at[b], at_z(i))

    def finish(b):
        t2[b, z] = t2s[b, z]
        d2[b, z] = d2s[b, z]
        arrive(t2.at[b, pl.ds(1, NZ - 1)], r_t2.at[b])
        stats = jnp.concatenate([t2[b, i] for i in range(NZ)], axis=0)
        largest = jnp.max(stats, axis=0, keepdims=True)
        factors = jnp.exp(stats - largest) * pltpu.roll(stats, LANES - 1, 1)
        summed = jnp.sum(factors, axis=0, keepdims=True)
        shares = factors / jnp.maximum(summed, 1.0)
        arrive(d2.at[b, pl.ds(1, NZ - 1)], r_d2.at[b])
        deep[b] = d2[b].astype(F32).reshape(NZ * ROWS, LANES)
        for h in range(HL):
            share = take(shares, 2 * h)
            for j in range(PARTS):
                rows = deep[b, pl.ds(h * PARTS + j, NZ, stride=ROWS)]
                row = jnp.sum(share * rows, axis=0, keepdims=True)
                lat[b * HL + h:b * HL + h + 1, j * LANES:(j + 1) * LANES] = row

    first_slot = kv * ctx
    late[2].wait()

    def scores_of(b):
        if b == LAST:
            turn()
            tail = qrope3[:, :ROPE]
        else:
            arrive(qall.at[b, pl.ds(0, HEADS - GROUP)], r_g2.at[b])
            if b == 0:
                arrive(qrope.at[pl.ds(0, HEADS - GROUP)], r_g2.at[LAST])
            tail = qrope[:, b * ROPE:(b + 1) * ROPE]
        scores = jnp.dot(
            qall[b], kvt[b, :RANK], preferred_element_type=F32
        ) + jnp.dot(tail, kvt[b, RANK:], preferred_element_type=F32)
        slot = lax.broadcasted_iota(jnp.int32, (1, ctx), 1)
        return jnp.where(slot < lengths[b] - first_slot, scores, DEAD)

    scores = scores_of(0)
    for b in range(B):
        following = scores_of(b + 1) if b + 1 < B else None
        m = jnp.max(scores, axis=1, keepdims=True)
        weights = jnp.exp2((scores - jnp.maximum(m, FLOOR)) * (scale * math.log2(math.e)))
        l = jnp.sum(weights, axis=1, keepdims=True)
        weights = weights.astype(BF16)
        inverse = 1.0 / jnp.maximum(l, 1.0)
        pack(b, m * scale, l)
        step = RANK // 2 if b == LAST else RANK
        for c in range(0, RANK, step):
            total = jnp.dot(weights, vt[b, :, c:c + step], preferred_element_type=F32)
            d1s[b, :, c:c + step] = (total * inverse).astype(BF16)
            for d in (2, 1, 3):
                i = ys(d)
                if c == 0:
                    send(t1s.at[b, i], t1.at[b, y], sent.at[5], r_t1.at[b], at_y(i))
                cols = pl.ds(c, step)
                send(
                    d1s.at[b, yrows(i), cols], d1.at[b, y, :, cols],
                    sent.at[4], r_d1.at[b], at_y(i),
                )
        scores = following
    for b in range(B):
        join(b)
    for b in range(B):
        finish(b)
    latent = lat[...].astype(BF16)

    late[0].wait()
    heads = jnp.zeros((ROWS, VH), F32)
    for h in range(HL):
        product = jnp.dot(latent, wuv[h], preferred_element_type=F32)
        heads = jnp.where(head == h, product, heads)
    fall[s] = heads.astype(BF16)
    for d in (4, 3, 5, 2, 6, 1, 7):
        send(fall.at[s], fall.at[s], sent.at[8], r_f, at_s(ss(d)))
    arrive(fall.at[pl.ds(1, NS - 1)], r_f)
    ff[...] = fall[...].astype(F32).reshape(NS * ROWS, VH)
    late[1].wait()
    x = jnp.concatenate(
        [
            jnp.concatenate(
                [ff[pl.ds(b * HL + h, NS, stride=ROWS)] for h in range(HL)], axis=1
            )
            for b in range(B)
        ],
        axis=0,
    ).astype(BF16)
    product = jnp.dot(x, wo[...], preferred_element_type=F32)
    pieces = product.shape[1] // LANES
    wide[...] = jnp.zeros(wide.shape, F32)
    for j in range(pieces):
        wide[pl.ds(j, SEQS, stride=8)] = product[:, j * LANES:(j + 1) * LANES]
    h2s[...] = wide[...].reshape(h2s.shape).astype(BF16)
    for dz, dy in sorted(
        ((dz, dy) for dz in range(NZ) for dy in range(NY) if dz or dy),
        key=lambda d: (-min(d[0], NZ - d[0]) - min(d[1], NY - d[1]), d),
    ):
        i, j = zs(dz), ys(dy)
        send(h2s.at[j * NZ + i], h2.at[kv], sent.at[9], r_h2, {"kv": i * NY + j, "seq": s})
    h2[kv] = h2s[y * NZ + z]
    arrive(h2.at[pl.ds(1, NZ * NY - 1)], r_h2)
    total = jnp.sum(h2[...].astype(F32), axis=0)
    out[...] = jnp.concatenate([total[j:j + 1] for j in range(pieces)], axis=1).astype(
        BF16
    )
    all_sent = [
        g1r.at[pl.ds(1, NZ - 1)],
        g1.at[pl.ds(1, NZ - 1), pl.ds(0, LAST)],
        qall.at[pl.ds(0, LAST), pl.ds(0, HEADS - GROUP)],
        qrope.at[pl.ds(0, HEADS - GROUP)],
        d1s.at[:, pl.ds(0, HEADS - GROUP)],
        t1s.at[:, pl.ds(1, NY - 1)],
        d2s.at[:, pl.ds(1, NZ - 1)],
        t2s.at[:, pl.ds(1, NZ - 1)],
        fall.at[pl.ds(1, NS - 1)],
        h2s.at[pl.ds(1, NZ * NY - 1)],
        ya.at[pl.ds(1, NY - 1)],
        za.at[pl.ds(1, NZ - 1)],
    ]
    for i, ref in enumerate(all_sent):
        bytes_of(ref, sent.at[i]).wait_send()


def per_device(kv_cache, lengths, q_nope, q_rope, w_uk, w_uv, w_o):
    ctx = kv_cache.shape[1]
    dmodel = w_o.shape[1]
    dma = pltpu.SemaphoreType.DMA
    anywhere = pl.BlockSpec(memory_space=pl.ANY)
    return pl.pallas_call(
        kernel,
        out_shape=jax.ShapeDtypeStruct((1, dmodel), BF16),
        in_specs=[anywhere] * 7,
        out_specs=pl.BlockSpec(memory_space=pltpu.VMEM),
        scratch_shapes=[
            pltpu.SMEM((B,), jnp.int32),
            pltpu.VMEM((B, HL, NOPE), BF16),
            pltpu.VMEM((B, HL, ROPE), BF16),
            pltpu.VMEM((B, RANK + ROPE, ctx), BF16),
            pltpu.VMEM((B, ctx, RANK), BF16),
            pltpu.VMEM((HL, NOPE, RANK), BF16),
            pltpu.VMEM((HL, RANK, VH), BF16),
            pltpu.VMEM((HL * VH, dmodel), BF16),
            pltpu.VMEM((ROWS * PARTS, LANES), F32),
            pltpu.VMEM((NZ, B, HL * PARTS, LANES), BF16),
            pltpu.VMEM((NZ, ROWS, LANES), BF16),
            pltpu.VMEM((NY, 2, ROWS, LANES), BF16),
            pltpu.VMEM((NZ, ROWS, RANK + LANES), BF16),
            pltpu.VMEM((B, GROUP * PARTS, LANES), F32),
            pltpu.VMEM((NY * ROWS, LANES), F32),
            pltpu.VMEM((B, HEADS, RANK), BF16),
            pltpu.VMEM((HEADS, B * ROPE), BF16),
            pltpu.VMEM((HEADS, LANES), BF16),
            pltpu.VMEM((B, HEADS, RANK), BF16),
            pltpu.VMEM((B, NY, GROUP, RANK), BF16),
            pltpu.VMEM((B, HEADS, LANES), F32),
            pltpu.VMEM((B, NY, NZ, LANES), F32),
            pltpu.VMEM((B, NY, NZ, LANES), F32),
            pltpu.VMEM((B, NY, GROUP, LANES), F32),
            pltpu.VMEM((B, GROUP * PARTS, LANES), F32),
            pltpu.VMEM((B, NZ, ROWS, LANES), BF16),
            pltpu.VMEM((B, NZ, ROWS, LANES), BF16),
            pltpu.VMEM((B, NZ, 1, LANES), F32),
            pltpu.VMEM((B, NZ, 1, LANES), F32),
            pltpu.VMEM((B, NZ * ROWS, LANES), F32),
            pltpu.VMEM((ROWS, RANK), F32),
            pltpu.VMEM((NS, ROWS, VH), BF16),
            pltpu.VMEM((NS * ROWS, VH), F32),
            pltpu.VMEM((SEQS * 8, LANES), F32),
            pltpu.VMEM((SEQS, 8, LANES), BF16),
            pltpu.VMEM((SEQS, 8, LANES), BF16),
            dma((6,)), dma((B,)), dma((12,)),
            dma((3,)), dma((B,)), dma((2,)),
            dma((B,)), dma((B,)), dma((B,)), dma((B,)),
            dma, dma,
        ],
        compiler_params=pltpu.CompilerParams(
            collective_id=0, has_side_effects=True, vmem_limit_bytes=62 * 1024 * 1024
        ),
    )(lengths, q_nope, q_rope, jnp.swapaxes(kv_cache, 1, 2), w_uk, w_uv, w_o)


def solution(mesh):
    return jax.shard_map(
        per_device,
        mesh=mesh,
        in_specs=(
            P("seq", "kv", None),
            P("seq"),
            P("seq", "kv", None),
            P("seq", "kv", None),
            P("kv", None, None),
            P("kv", None, None),
            P("kv", "seq"),
        ),
        out_specs=P("kv", "seq"),
        check_vma=False,
    )
```

time: 316 us -> 45.2 us (0.14)
  the two profiles are of different devices: /device:TPU:2 before, /device:TPU:1 now
where the time goes in v1:
time: 45.2 us; the launch traced here: 45 us
  Pallas kernels  43.7 us (97%)
  local copies, waits for them, and re-layouts  1.27 us (3%)
    pallas_call x1, Pallas kernels, per_device(): pl.pallas_call(kernel, out_shape=jax.ShapeDtypeStruct((1, dmodel), BF16),...  43.7 us
    unnamed x1, local copies, waits for them, and re-layouts  1.27 us

profile of v1, /device:TPU:1, one launch (start us, length us, event | category | flops | bytes accessed | tf_op | source)
XLA Modules:
  0.0 45.0 jit_solution(15356450342511368635)
XLA Ops:
  0.0 43.7 %shard_map.73 = bf16[1,896]{1,0:T(2,128)(2,1)} custom-call(s32[4]{0:T(128)} %lengths_hbm.1, bf16[4,4,128]{2,1,0:T(4,128)(2,1)} %qn_hbm.1, bf16[4,4,64]{2,1,0:T(4,128)(2,1)} %qr_hbm.1, bf16[4,576,2304]{2,1,0:T(8,128)(2,1)} %bitcast.1, bf16[4,128,512]{2,1,0:T(8,128)(2,1)} %wuk_hbm.1, bf16[4,512,128]{2,1,0:T(8,128)(2,1)} %wuv_hbm.1, bf16[512,896]{1,0:T(8,128)(2,1)} %wo_hbm.1), custom_call_target="tpu_custom_call" | custom-call | tf_op jit(solution)/shard_map/pallas_call | solution.py:371
  43.8 1.3 %copy.9 = bf16[1,896]{1,0:T(2,128)(2,1)} copy(bf16[1,896]{1,0:T(2,128)(2,1)} %shard_map.73) | data formatting | bytes 3584

commit v2 on v1

--- a/solution.py
+++ b/solution.py
@@ -39,9 +39,9 @@
 def kernel(
     lengths_hbm, qn_hbm, qr_hbm, kv_hbm, wuk_hbm, wuv_hbm, wo_hbm, out,
     lengths, qn, qr, kvt, vt, wuk, wuv, wo,
-    own, g1, g1r, ya, za, spread, around, qall, qrope, qrope3, d1s, d1, tall, t1s, t1, factor, flat, d2s, d2, t2s, t2, deep,
+    own, g1, g1r, ya, za, spread, around, qall, qrope, qrope3, e1s, e1, u1s, u1, fz, f2, e2s, e2, u2s, u2, d1s, d1, tall, t1s, t1, factor, flat, d2s, d2, t2s, t2, deep,
     lat, fall, ff, wide, h2s, h2,
-    local, local_kv, sent, r_g1, r_g2, r_a, r_d1, r_t1, r_d2, r_t2, r_f, r_h2,
+    local, local_kv, sent, r_g1, r_g2, r_a, r_e, r_d1, r_t1, r_d2, r_t2, r_f, r_h2,
 ):
     kv, s = lax.axis_index("kv"), lax.axis_index("seq")
     z, y = kv // NY, kv % NY
@@ -211,6 +211,72 @@
                 block = block + pltpu.roll(tall[b, pl.ds(i * GROUP + h, NZ, stride=HL)], 2 * h, 1)
             t1s[b, i] = block
 
+    def pack_z(maxima, totals):
+        lane = lax.broadcasted_iota(jnp.int32, (HEADS, LANES), 1)
+        tall[0] = jnp.where(lane == 0, maxima, jnp.where(lane == 1, totals, 0.0))
+        block = tall[0, pl.ds(0, NZ, stride=HL)]
+        for r in range(1, ROWS):
+            first = (r // HL) * GROUP + r % HL
+            block = block + pltpu.roll(tall[0, pl.ds(first, NZ, stride=HL)], 2 * r, 1)
+        for i in range(NZ):
+            u1s[i] = block[i:i + 1]
+
+    def leave_z(outputs):
+        for k in range(NZ // 2):
+            blocks = [outputs[i * GROUP + 8 * k:i * GROUP + 8 * k + 8] for i in range(NY)]
+            low, high = halves(blocks[0], blocks[1]), halves(blocks[2], blocks[3])
+            for i in range(2):
+                e1s[2 * k + i] = jnp.concatenate([low[i], high[i]], axis=0).astype(BF16)
+        for d in FAR_FIRST:
+            i = zs(d)
+            send(u1s.at[i], u1.at[z], sent.at[12], r_e.at[0], at_z(i))
+            send(e1s.at[i], e1.at[z], sent.at[13], r_e.at[1], at_z(i))
+
+    def join_z():
+        u1[z] = u1s[z]
+        e1[z] = e1s[z]
+        arrive(u1.at[pl.ds(1, NZ - 1)], r_e.at[0])
+        stats = jnp.concatenate([u1[i] for i in range(NZ)], axis=0)
+        largest = jnp.broadcast_to(jnp.max(stats, axis=0, keepdims=True), stats.shape)
+        factors = jnp.exp(stats - largest) * pltpu.roll(stats, LANES - 1, 1)
+        summed = jnp.broadcast_to(jnp.sum(factors, axis=0, keepdims=True), stats.shape)
+        shares = factors / jnp.maximum(summed, 1.0)
+        u2s[...] = jnp.where(even, largest, pltpu.roll(summed, 1, 1))[:1]
+        for r in range(ROWS):
+            fz[pl.ds(r, NZ, stride=ROWS)] = take(shares, 2 * r)
+        arrive(e1.at[pl.ds(1, NZ - 1)], r_e.at[1])
+        total = 0.0
+        for i in range(NZ):
+            share = jnp.concatenate([fz[i * ROWS:(i + 1) * ROWS]] * PARTS, axis=1)
+            total = total + share * e1[i].astype(F32)
+        for j in range(PARTS):
+            f2[pl.ds(j, ROWS, stride=PARTS)] = total[:, j * LANES:(j + 1) * LANES]
+        e2s[...] = f2[...].astype(BF16).reshape(NY, ROWS, LANES)
+        for d in (2, 1, 3):
+            i = ys(d)
+            send(u2s, u2.at[y], sent.at[14], r_e.at[2], at_y(i))
+            send(e2s.at[i], e2.at[y], sent.at[15], r_e.at[3], at_y(i))
+
+    def finish_z():
+        u2[y] = u2s[...]
+        e2[y] = e2s[y]
+        arrive(u2.at[pl.ds(1, NY - 1)], r_e.at[2])
+        rows = [u2[i] for i in range(NY)] + [jnp.full((NZ - NY, LANES), DEAD, F32)]
+        stats = jnp.concatenate(rows, axis=0)
+        stats = pltpu.roll(stats, lax.rem(LANES - 2 * HL * y, LANES), 1)
+        largest = jnp.max(stats, axis=0, keepdims=True)
+        factors = jnp.exp(stats - largest) * pltpu.roll(stats, LANES - 1, 1)
+        summed = jnp.sum(factors, axis=0, keepdims=True)
+        shares = factors / jnp.maximum(summed, 1.0)
+        arrive(e2.at[pl.ds(1, NY - 1)], r_e.at[3])
+        f2[...] = e2[...].astype(F32).reshape(NY * ROWS, LANES)
+        for h in range(HL):
+            share = take(shares, 2 * h)[:NY]
+            for j in range(PARTS):
+                rows = f2[pl.ds(h * PARTS + j, NY, stride=ROWS)]
+                row = jnp.sum(share * rows, axis=0, keepdims=True)
+                lat[h:h + 1, j * LANES:(j + 1) * LANES] = row
+
     def join(b):
         t1[b, y] = t1s[b, y]
         d1[b, y] = d1s[b, yrows(y)]
@@ -286,6 +352,11 @@
         l = jnp.sum(weights, axis=1, keepdims=True)
         weights = weights.astype(BF16)
         inverse = 1.0 / jnp.maximum(l, 1.0)
+        if b == 0:
+            pack_z(m * scale, l)
+            leave_z(jnp.dot(weights, vt[0], preferred_element_type=F32) * inverse)
+            scores = following
+            continue
         pack(b, m * scale, l)
         step = RANK // 2 if b == LAST else RANK
         for c in range(0, RANK, step):
@@ -301,44 +372,62 @@
                     sent.at[4], r_d1.at[b], at_y(i),
                 )
         scores = following
-    for b in range(B):
+    for b in range(1, B):
         join(b)
-    for b in range(B):
+    join_z()
+    wide[...] = jnp.zeros(wide.shape, F32)
+    lat[LAST * HL:] = jnp.zeros((HL, RANK), F32)
+    pieces = wo.shape[1] // LANES
+
+    def values(part):
+        latent = lat[...].astype(BF16)
+        heads = jnp.zeros((ROWS, VH), F32)
+        for h in range(HL):
+            product = jnp.dot(latent, wuv[h], preferred_element_type=F32)
+            heads = jnp.where(head == h, product, heads)
+        fall[part, s] = heads.astype(BF16)
+        for d in (4, 3, 5, 2, 6, 1, 7):
+            send(fall.at[part, s], fall.at[part, s], sent.at[8], r_f.at[part], at_s(ss(d)))
+
+    def project(part, some):
+        arrive(fall.at[part, pl.ds(1, NS - 1)], r_f.at[part])
+        ff[part] = fall[part].astype(F32).reshape(NS * ROWS, VH)
+        x = [
+            jnp.concatenate(
+                [ff[part, pl.ds(b * HL + h, NS, stride=ROWS)] for h in range(HL)], axis=1
+            )
+            for b in some
+        ]
+        product = jnp.dot(
+            jnp.concatenate(x, axis=0).astype(BF16), wo[...], preferred_element_type=F32
+        )
+        first, count = some[0] * NS, len(some) * NS
+        for j in range(pieces):
+            wide[pl.ds(first * 8 + j, count, stride=8)] = product[:, j * LANES:(j + 1) * LANES]
+        rows = wide[first * 8:(first + count) * 8]
+        h2s[first:first + count] = rows.reshape(count, 8, LANES).astype(BF16)
+
+        def give(b, dz):
+            i = zs(dz)
+            to = {"kv": i * NY + b, "seq": s}
+            send(h2s.at[b * NZ + i], h2.at[kv], sent.at[9], r_h2, to)
+
+        for dz in FAR_FIRST:
+            for b in some:
+                give(b, dz)
+        for b in some:
+            pl.when(y != b)(functools.partial(give, b, 0))
+
+    for b in range(1, LAST):
         finish(b)
-    latent = lat[...].astype(BF16)
-
+    finish_z()
     late[0].wait()
-    heads = jnp.zeros((ROWS, VH), F32)
-    for h in range(HL):
-        product = jnp.dot(latent, wuv[h], preferred_element_type=F32)
-        heads = jnp.where(head == h, product, heads)
-    fall[s] = heads.astype(BF16)
-    for d in (4, 3, 5, 2, 6, 1, 7):
-        send(fall.at[s], fall.at[s], sent.at[8], r_f, at_s(ss(d)))
-    arrive(fall.at[pl.ds(1, NS - 1)], r_f)
-    ff[...] = fall[...].astype(F32).reshape(NS * ROWS, VH)
+    values(0)
+    finish(LAST)
+    values(1)
     late[1].wait()
-    x = jnp.concatenate(
-        [
-            jnp.concatenate(
-                [ff[pl.ds(b * HL + h, NS, stride=ROWS)] for h in range(HL)], axis=1
-            )
-            for b in range(B)
-        ],
-        axis=0,
-    ).astype(BF16)
-    product = jnp.dot(x, wo[...], preferred_element_type=F32)
-    pieces = product.shape[1] // LANES
-    wide[...] = jnp.zeros(wide.shape, F32)
-    for j in range(pieces):
-        wide[pl.ds(j, SEQS, stride=8)] = product[:, j * LANES:(j + 1) * LANES]
-    h2s[...] = wide[...].reshape(h2s.shape).astype(BF16)
-    for dz, dy in sorted(
-        ((dz, dy) for dz in range(NZ) for dy in range(NY) if dz or dy),
-        key=lambda d: (-min(d[0], NZ - d[0]) - min(d[1], NY - d[1]), d),
-    ):
-        i, j = zs(dz), ys(dy)
-        send(h2s.at[j * NZ + i], h2.at[kv], sent.at[9], r_h2, {"kv": i * NY + j, "seq": s})
+    project(0, range(LAST))
+    project(1, [LAST])
     h2[kv] = h2s[y * NZ + z]
     arrive(h2.at[pl.ds(1, NZ * NY - 1)], r_h2)
     total = jnp.sum(h2[...].astype(F32), axis=0)
@@ -350,14 +439,18 @@
         g1.at[pl.ds(1, NZ - 1), pl.ds(0, LAST)],
         qall.at[pl.ds(0, LAST), pl.ds(0, HEADS - GROUP)],
         qrope.at[pl.ds(0, HEADS - GROUP)],
-        d1s.at[:, pl.ds(0, HEADS - GROUP)],
-        t1s.at[:, pl.ds(1, NY - 1)],
-        d2s.at[:, pl.ds(1, NZ - 1)],
-        t2s.at[:, pl.ds(1, NZ - 1)],
-        fall.at[pl.ds(1, NS - 1)],
+        d1s.at[pl.ds(1, LAST), pl.ds(0, HEADS - GROUP)],
+        t1s.at[pl.ds(1, LAST), pl.ds(1, NY - 1)],
+        d2s.at[pl.ds(1, LAST), pl.ds(1, NZ - 1)],
+        t2s.at[pl.ds(1, LAST), pl.ds(1, NZ - 1)],
+        fall.at[:, pl.ds(1, NS - 1)],
         h2s.at[pl.ds(1, NZ * NY - 1)],
         ya.at[pl.ds(1, NY - 1)],
         za.at[pl.ds(1, NZ - 1)],
+        u1s.at[pl.ds(1, NZ - 1)],
+        e1s.at[pl.ds(1, NZ - 1)],
+        u2.at[pl.ds(1, NY - 1)],
+        e2s.at[pl.ds(1, NY - 1)],
     ]
     for i, ref in enumerate(all_sent):
         bytes_of(ref, sent.at[i]).wait_send()
@@ -392,6 +485,16 @@
             pltpu.VMEM((B, HEADS, RANK), BF16),
             pltpu.VMEM((HEADS, B * ROPE), BF16),
             pltpu.VMEM((HEADS, LANES), BF16),
+            pltpu.VMEM((NZ, ROWS, RANK), BF16),
+            pltpu.VMEM((NZ, ROWS, RANK), BF16),
+            pltpu.VMEM((NZ, 1, LANES), F32),
+            pltpu.VMEM((NZ, 1, LANES), F32),
+            pltpu.VMEM((NZ * ROWS, LANES), F32),
+            pltpu.VMEM((NY * ROWS, LANES), F32),
+            pltpu.VMEM((NY, ROWS, LANES), BF16),
+            pltpu.VMEM((NY, ROWS, LANES), BF16),
+            pltpu.VMEM((1, LANES), F32),
+            pltpu.VMEM((NY, 1, LANES), F32),
             pltpu.VMEM((B, HEADS, RANK), BF16),
             pltpu.VMEM((B, NY, GROUP, RANK), BF16),
             pltpu.VMEM((B, HEADS, LANES), F32),
@@ -405,15 +508,15 @@
             pltpu.VMEM((B, NZ, 1, LANES), F32),
             pltpu.VMEM((B, NZ * ROWS, LANES), F32),
             pltpu.VMEM((ROWS, RANK), F32),
-            pltpu.VMEM((NS, ROWS, VH), BF16),
-            pltpu.VMEM((NS * ROWS, VH), F32),
+            pltpu.VMEM((2, NS, ROWS, VH), BF16),
+            pltpu.VMEM((2, NS * ROWS, VH), F32),
             pltpu.VMEM((SEQS * 8, LANES), F32),
             pltpu.VMEM((SEQS, 8, LANES), BF16),
             pltpu.VMEM((SEQS, 8, LANES), BF16),
-            dma((6,)), dma((B,)), dma((12,)),
-            dma((3,)), dma((B,)), dma((2,)),
+            dma((6,)), dma((B,)), dma((16,)),
+            dma((3,)), dma((B,)), dma((2,)), dma((4,)),
             dma((B,)), dma((B,)), dma((B,)), dma((B,)),
-            dma, dma,
+            dma((2,)), dma,
         ],
         compiler_params=pltpu.CompilerParams(
             collective_id=0, has_side_effects=True, vmem_limit_bytes=62 * 1024 * 1024

time: 45.2 us -> 44.1 us (0.976)
  Pallas kernels: 43.7 us -> 42.6 us
    pallas_call x1, Pallas kernels: 43.7 us -> 42.6 us  [per_device(): pl.pallas_call(kernel, out_shape=jax.ShapeDtypeStruct((1, dmodel), BF16),...]
where the time goes in v2:
time: 44.1 us; the launch traced here: 43.9 us
  Pallas kernels  42.6 us (97%)
  local copies, waits for them, and re-layouts  1.27 us (3%)
    pallas_call x1, Pallas kernels, per_device(): pl.pallas_call(kernel, out_shape=jax.ShapeDtypeStruct((1, dmodel), BF16),...  42.6 us
    unnamed x1, local copies, waits for them, and re-layouts  1.27 us

profile of v2, /device:TPU:1, one launch (start us, length us, event | category | flops | bytes accessed | tf_op | source)
XLA Modules:
  0.0 43.9 jit_solution(9761766568122717368)
XLA Ops:
  0.0 42.6 %shard_map.73 = bf16[1,896]{1,0:T(2,128)(2,1)} custom-call(s32[4]{0:T(128)} %lengths_hbm.1, bf16[4,4,128]{2,1,0:T(4,128)(2,1)} %qn_hbm.1, bf16[4,4,64]{2,1,0:T(4,128)(2,1)} %qr_hbm.1, bf16[4,576,2304]{2,1,0:T(8,128)(2,1)} %bitcast.1, bf16[4,128,512]{2,1,0:T(8,128)(2,1)} %wuk_hbm.1, bf16[4,512,128]{2,1,0:T(8,128)(2,1)} %wuv_hbm.1, bf16[512,896]{1,0:T(8,128)(2,1)} %wo_hbm.1), custom_call_target="tpu_custom_call" | custom-call | tf_op jit(solution)/shard_map/pallas_call | solution.py:464
  42.7 1.3 %copy.9 = bf16[1,896]{1,0:T(2,128)(2,1)} copy(bf16[1,896]{1,0:T(2,128)(2,1)} %shard_map.73) | data formatting | bytes 3584

commit v3 on v2

--- a/solution.py
+++ b/solution.py
@@ -429,11 +429,6 @@
     project(0, range(LAST))
     project(1, [LAST])
     h2[kv] = h2s[y * NZ + z]
-    arrive(h2.at[pl.ds(1, NZ * NY - 1)], r_h2)
-    total = jnp.sum(h2[...].astype(F32), axis=0)
-    out[...] = jnp.concatenate([total[j:j + 1] for j in range(pieces)], axis=1).astype(
-        BF16
-    )
     all_sent = [
         g1r.at[pl.ds(1, NZ - 1)],
         g1.at[pl.ds(1, NZ - 1), pl.ds(0, LAST)],
@@ -454,6 +449,11 @@
     ]
     for i, ref in enumerate(all_sent):
         bytes_of(ref, sent.at[i]).wait_send()
+    arrive(h2.at[pl.ds(1, NZ * NY - 1)], r_h2)
+    total = jnp.sum(h2[...].astype(F32), axis=0)
+    out[...] = jnp.concatenate([total[j:j + 1] for j in range(pieces)], axis=1).astype(
+        BF16
+    )
 
 
 def per_device(kv_cache, lengths, q_nope, q_rope, w_uk, w_uv, w_o):

time: 44.1 us -> 44.1 us (level)
  no operation moved by 1% of the time
where the time goes in v3:
time: 44.1 us; the launch traced here: 43.9 us
  Pallas kernels  42.6 us (97%)
  local copies, waits for them, and re-layouts  1.27 us (3%)
    pallas_call x1, Pallas kernels, per_device(): pl.pallas_call(kernel, out_shape=jax.ShapeDtypeStruct((1, dmodel), BF16),...  42.6 us
    unnamed x1, local copies, waits for them, and re-layouts  1.27 us

profile of v3, /device:TPU:1, one launch (start us, length us, event | category | flops | bytes accessed | tf_op | source)
XLA Modules:
  0.0 43.9 jit_solution(2511816157870179674)
XLA Ops:
  0.0 42.6 %shard_map.73 = bf16[1,896]{1,0:T(2,128)(2,1)} custom-call(s32[4]{0:T(128)} %lengths_hbm.1, bf16[4,4,128]{2,1,0:T(4,128)(2,1)} %qn_hbm.1, bf16[4,4,64]{2,1,0:T(4,128)(2,1)} %qr_hbm.1, bf16[4,576,2304]{2,1,0:T(8,128)(2,1)} %bitcast.1, bf16[4,128,512]{2,1,0:T(8,128)(2,1)} %wuk_hbm.1, bf16[4,512,128]{2,1,0:T(8,128)(2,1)} %wuv_hbm.1, bf16[512,896]{1,0:T(8,128)(2,1)} %wo_hbm.1), custom_call_target="tpu_custom_call" | custom-call | tf_op jit(solution)/shard_map/pallas_call | solution.py:464
  42.6 1.3 %copy.9 = bf16[1,896]{1,0:T(2,128)(2,1)} copy(bf16[1,896]{1,0:T(2,128)(2,1)} %shard_map.73) | data formatting | bytes 3584
